TPU v7x, 128 devices: a whole 4x4x4 slice. The times are simulated.
128 devices in a mesh: sx: 8 (over x, z_lo), sy: 16 (over y, z_hi, core).
Axes of the slice: x: 4, y: 4, z: 4 (z_hi: 2, z_lo: 2; z = z_hi * 2 + z_lo), core: 2. Of those that a mesh axis runs over, the one named last changes fastest.
Arguments:
- signal: bfloat16 [8, 16, 1024, 512], P('sx', 'sy'), may hold values from -6 to 6
- box_phase: float32 [13, 8, 16, 256], P(None, 'sx', 'sy'), may hold values from -3.140625 to 3.140625
- node_phase: float32 [13, 1024, 256], replicated, may hold values from -3.140625 to 3.140625
- local_interp: bfloat16 [2, 2, 2, 256, 256], replicated, may hold values from -0.1875 to 0.1875
- across_x: bfloat16 [2, 2, 2, 256, 256], replicated, may hold values from -0.1875 to 0.1875
- across_y: bfloat16 [2, 2, 2, 256, 256], replicated, may hold values from -0.1875 to 0.1875
Outputs:
- spectrum: bfloat16 [8, 16, 1024, 512], P('sx', 'sy')
All inputs are finite; a program needn't handle non-finite values.
Results may differ from a plain program's by a relative error of at most 0.04.
Values may be sent and summed in bfloat16 or wider, within the bound.
No kernel may reach another device: no remote copies, remote signals or barrier semaphores. Data moves between devices by JAX's collectives and lax.ppermute only.
A program may use at most 128 MiB of HBM per device.

v0:
```python
import functools

import jax
import jax.numpy as jnp
from jax import lax
from jax.experimental import pallas as pl
from jax.experimental.pallas import tpu as pltpu
from jax.sharding import PartitionSpec as P

AXES = ("sx", "sy")
ROWS = 1024
NODES = 256
WIDTH = 512
BOXES = 128
SLAB = 8
CHUNK = 64
HALF = ROWS // 2
STRIP = 128
CODE = 38.0
MESSAGE = 48
DATA = 32
FIRST = 1
INNER = 9
LAST = FIRST + INNER
WITHIN = 2
BLOCK = 256
BOX_BITS = (4, 0, 5, 1, 6, 2, 3)
SECOND = (0, 1, 0, 1, 0, 1, 1)
SPLITS = (6, 6, 6, 5, 5, 5, 5)
SPLIT = 6

SIN = (9.99999242e-01, -1.66656797e-01, 8.31322541e-03, -1.85234428e-04)
COS = (0.99999325, -0.49991211, 0.04148738, -0.00127111)


def horner(coefficients, x):
    total = coefficients[-1] * x + coefficients[-2]
    for factor in coefficients[-3::-1]:
        total = total * x + factor
    return total


def cos_sin(angle):
    half = angle * 0.5
    square = half * half
    sine = half * horner(SIN, square)
    cosine = horner(COS, square)
    double = sine + sine
    return 1.0 - double * sine, double * cosine


def pair_slabs(bit, half, split, block):
    return [
        slab
        for slab in range(BOXES)
        if slab >> bit & 1 == half and slab >> split & 1 == block
    ]


def runs(slabs):
    found = []
    for i, slab in enumerate(slabs):
        if found and found[-1][1] + found[-1][2] == slab * SLAB:
            found[-1][2] += SLAB
        else:
            found.append([i * SLAB, slab * SLAB, SLAB])
    return found


def load_slabs(ref, slabs, columns):
    parts = [ref[r : r + n, columns] for _, r, n in runs(slabs)]
    return parts[0] if len(parts) == 1 else jnp.concatenate(parts, axis=0)


def interleave(major, minor):
    done = 0
    for i, step in enumerate(major):
        step()
        upto = len(minor) * (i + 1) // len(major)
        for other in minor[done:upto]:
            other()
        done = upto
    for other in minor[done:]:
        other()


def pipeline(levels, rotate, multiply, apart=()):
    stages = [(k, block) for k in range(levels) for block in range(2)]
    ready = rotate(*stages[0])
    for i, stage in enumerate(stages):
        if i == 0 or stage in apart:
            interleave(ready, [])
        after = stages[i + 1] if i + 1 < len(stages) else None
        ready = rotate(*after) if after else []
        interleave(multiply(*stage), [] if after in apart else ready)


RE = slice(0, NODES)
IM = slice(NODES, WIDTH)


VMEM = pl.BlockSpec(memory_space=pltpu.VMEM)
HBM = pl.BlockSpec(memory_space=pltpu.HBM)
DMA = pltpu.SemaphoreType.DMA


def fill_weight(weight, interp):
    for child in range(2):
        for source in range(2):
            r, c = source * WIDTH, child * WIDTH
            real, imag = interp[child, source, 0], interp[child, source, 1]
            weight[r : r + NODES, c : c + NODES] = real
            weight[r : r + NODES, c + NODES : c + WIDTH] = imag
            weight[r + NODES : r + WIDTH, c : c + NODES] = -imag
            weight[r + NODES : r + WIDTH, c + NODES : c + WIDTH] = real


def product(mixed, block, part, weight):
    return jnp.dot(
        mixed[block * BLOCK : (block + 1) * BLOCK],
        weight[:, part * NODES : (part + 1) * NODES],
        preferred_element_type=jnp.float32,
    )


def strip(j):
    return slice(j * STRIP, (j + 1) * STRIP)


def rotate_into(mixed, rows, half, re, im, c, s):
    left = half * WIDTH
    mixed[rows, left : left + NODES] = (re * c - im * s).astype(jnp.bfloat16)
    mixed[rows, left + NODES : left + WIDTH] = (re * s + im * c).astype(jnp.bfloat16)


def swap(bit, zero, one):
    distance = 1 << bit
    at_zero = lax.broadcasted_iota(jnp.int32, zero.shape, 1) & distance == 0
    return (
        jnp.where(at_zero, zero, pltpu.roll(one, distance, 1)),
        jnp.where(at_zero, pltpu.roll(zero, SLAB - distance, 1), one),
    )


def mix_within(bit, block, i, j, sides, mixed):
    at = block * BLOCK + i * CHUNK
    for part in range(2):
        pair = [side[part].reshape(CHUNK // SLAB, SLAB, STRIP) for side in sides]
        for half, rows in enumerate(swap(bit, *pair)):
            mixed[at : at + CHUNK, strip(4 * half + 2 * part + j)] = rows.reshape(
                CHUNK, STRIP
            ).astype(jnp.bfloat16)


def multiply_within(bit, block, part, target, mixed, weight):
    pair = [
        product(mixed, block, 2 * child + part, weight).reshape(BLOCK // SLAB, SLAB, NODES)
        for child in range(2)
    ]
    for side, rows in enumerate(swap(bit, *pair)):
        first = block * HALF + side * BLOCK
        target[first : first + BLOCK, (RE, IM)[part]] = rows.reshape(BLOCK, NODES)


def first_kernel(
    data_hbm, box_ref, node_hbm, interp_hbm, out_hbm,
    data, nodes, interp, weight, cosines, sines, current, mixed, messages, sems,
):
    copies = [
        pltpu.make_async_copy(node_hbm.at[0], nodes, sems.at[0]),
        pltpu.make_async_copy(interp_hbm, interp, sems.at[1]),
        pltpu.make_async_copy(data_hbm, data, sems.at[2]),
    ]
    for copy in copies:
        copy.start()
    box_cos, box_sin = cos_sin(box_ref[0])
    next_cos, next_sin = cos_sin(box_ref[1])
    phases = [box_ref[FIRST + 1 + k][:, strip(j)] for j in range(2) for k in range(SLAB)]
    code = jnp.exp2(jnp.concatenate(phases, axis=0) * CODE).astype(jnp.bfloat16)
    messages[:, DATA:, :] = jnp.broadcast_to(code[None], (BOXES, 2 * SLAB, STRIP))
    copies[0].wait()
    for first in range(0, ROWS, CHUNK):
        for j in range(2):
            rows, columns = slice(first, first + CHUNK), strip(j)
            node_cos, node_sin = cos_sin(nodes[rows, columns])
            c, s = box_cos[:, columns], box_sin[:, columns]
            cosines[rows, columns] = node_cos * c - node_sin * s
            sines[rows, columns] = node_sin * c + node_cos * s
    copies[1].wait()
    fill_weight(weight, interp)
    copies[2].wait()

    def rotate_rows(block, i, j):
        sides = []
        for side in range(2):
            first = block * HALF + side * BLOCK + i * CHUNK
            rows = slice(first, first + CHUNK)
            c, s = cosines[rows, strip(j)], sines[rows, strip(j)]
            re = data[rows, strip(j)].astype(jnp.float32)
            im = data[rows, strip(2 + j)].astype(jnp.float32)
            sides.append((re * c - im * s, re * s + im * c))
        mix_within(0, block, i, j, sides, mixed)

    def rotate(k, block):
        return [
            functools.partial(rotate_rows, block, i, j)
            for i in range(BLOCK // CHUNK)
            for j in range(2)
        ]

    def pack(block, i):
        first = block * HALF + i * CHUNK
        rows, slabs = slice(first, first + CHUNK), slice(first // SLAB, (first + CHUNK) // SLAB)
        turned = []
        for j in range(2):
            c, s = next_cos[:, strip(j)], next_sin[:, strip(j)]
            re, im = current[rows, strip(j)], current[rows, strip(2 + j)]
            turned.append((re * c - im * s, re * s + im * c))
        for part in range(2):
            pair = [turned[j][part].reshape(CHUNK // SLAB, SLAB, STRIP) for j in range(2)]
            messages[slabs, 2 * SLAB * part : 2 * SLAB * (part + 1), :] = jnp.concatenate(
                pair, axis=1
            ).astype(jnp.bfloat16)

    leaving = [
        pltpu.make_async_copy(
            messages.at[pl.ds(block * CHUNK, CHUNK)],
            out_hbm.at[pl.ds(block * CHUNK, CHUNK)],
            sems.at[3 + block],
        )
        for block in range(2)
    ]

    def multiply(k, block):
        steps = [
            functools.partial(multiply_within, 0, block, part, current, mixed, weight)
            for part in range(2)
        ]
        steps += [functools.partial(pack, block, i) for i in range(HALF // CHUNK)]
        return steps + [leaving[block].start]

    pipeline(1, rotate, multiply)
    for copy in leaving:
        copy.wait()


def first_levels(data, box_phase, node_phase, interp):
    return pl.pallas_call(
        first_kernel,
        in_specs=[HBM, VMEM, HBM, HBM],
        out_specs=HBM,
        out_shape=jax.ShapeDtypeStruct((BOXES, MESSAGE, STRIP), jnp.bfloat16),
        scratch_shapes=[
            pltpu.VMEM((ROWS, WIDTH), jnp.bfloat16),
            pltpu.VMEM((ROWS, NODES), jnp.float32),
            pltpu.VMEM((2, 2, 2, NODES, NODES), jnp.bfloat16),
            pltpu.VMEM((2 * WIDTH, 2 * WIDTH), jnp.bfloat16),
            pltpu.VMEM((ROWS, NODES), jnp.float32),
            pltpu.VMEM((ROWS, NODES), jnp.float32),
            pltpu.VMEM((ROWS, WIDTH), jnp.float32),
            pltpu.VMEM((ROWS // 2, 2 * WIDTH), jnp.bfloat16),
            pltpu.VMEM((BOXES, MESSAGE, STRIP), jnp.bfloat16),
            DMA((5,)),
        ],
        compiler_params=pltpu.CompilerParams(vmem_limit_bytes=58 << 20),
        cost_estimate=pl.CostEstimate(flops=1 << 30, bytes_accessed=8 << 20, transcendentals=0),
        name="level0",
    )(data, box_phase, node_phase, interp)


def prep_kernel(
    box_ref, node_hbm, local_hbm, x_hbm, y_hbm,
    cos_ref, sin_ref, own_cos, own_sin, local_weight, inner_weight, x_weight, y_weight,
    own, nodes, interps, sems,
):
    me = lax.axis_index("sx") * lax.axis_size("sy") + lax.axis_index("sy")
    rows = pl.ds(pl.multiple_of(me * SLAB, SLAB), SLAB)
    copies = [
        pltpu.make_async_copy(node_hbm.at[pl.ds(FIRST, INNER), rows, :], own, sems.at[0]),
    ] + [pltpu.make_async_copy(node_hbm.at[LAST + k], nodes.at[k], sems.at[1 + k]) for k in range(3)]
    copies += [
        pltpu.make_async_copy(hbm, interps.at[k], sems.at[4 + k])
        for k, hbm in enumerate((x_hbm, y_hbm, local_hbm))
    ]
    for copy in copies:
        copy.start()
    copies[0].wait()
    own_cos[...], own_sin[...] = cos_sin(own[...])
    for k, weight in enumerate((x_weight, y_weight, local_weight)):
        copies[4 + k].wait()
        fill_weight(weight, interps.at[k])
    fill_weight(inner_weight, interps.at[2])
    for k in range(3):
        copies[1 + k].wait()
        box_cos, box_sin = cos_sin(box_ref[LAST + k])
        for half in range(2):
            for block in range(2):
                slabs = pair_slabs(k, half, SPLIT, block)
                for i in range(0, len(slabs), SLAB):
                    angles = load_slabs(nodes.at[k], slabs[i : i + SLAB], slice(None))
                    node_cos, node_sin = cos_sin(angles)
                    at = half * HALF + block * BLOCK + i * SLAB
                    cosine = node_cos * box_cos - node_sin * box_sin
                    sine = node_sin * box_cos + node_cos * box_sin
                    cos_ref[k, at : at + CHUNK, :] = cosine.astype(jnp.bfloat16)
                    sin_ref[k, at : at + CHUNK, :] = sine.astype(jnp.bfloat16)


def prep(box_phase, node_phase, *interps):
    weight = jax.ShapeDtypeStruct((2 * WIDTH, 2 * WIDTH), jnp.bfloat16)
    table = jax.ShapeDtypeStruct((3, ROWS, NODES), jnp.bfloat16)
    own = jax.ShapeDtypeStruct((INNER, SLAB, NODES), jnp.float32)
    return pl.pallas_call(
        prep_kernel,
        in_specs=[VMEM] + [HBM] * 4,
        out_specs=[VMEM] * 8,
        out_shape=[table, table, own, own, weight, weight, weight, weight],
        scratch_shapes=[
            pltpu.VMEM((INNER, SLAB, NODES), jnp.float32),
            pltpu.VMEM((3, ROWS, NODES), jnp.float32),
            pltpu.VMEM((3, 2, 2, 2, NODES, NODES), jnp.bfloat16),
            DMA((7,)),
        ],
        compiler_params=pltpu.CompilerParams(vmem_limit_bytes=52 << 20),
        cost_estimate=pl.CostEstimate(flops=60_000_000, bytes_accessed=7 << 20, transcendentals=0),
        name="prep",
    )(box_phase, node_phase, *interps)


def multiply_part(bit, split, block, part, target, mixed, weight):
    total = product(mixed, block, part, weight)
    for at, r, n in runs(pair_slabs(bit, part >> 1, split, block)):
        target[r : r + n, (RE, IM)[part & 1]] = total[at : at + n].astype(target.dtype)


def inner_kernel(
    data_ref, own_cos, own_sin, local_hbm, x_hbm, y_hbm, out_ref,
    current, mixed, box_cos, box_sin, weights, sems,
):
    copies = [
        pltpu.make_async_copy(hbm, weights.at[i], sems.at[i])
        for i, hbm in enumerate((local_hbm, x_hbm, y_hbm))
    ]
    copies[0].start()

    def receive(block, part):
        boxes = slice(block * CHUNK, (block + 1) * CHUNK)
        if part == 2:
            phase = jnp.log2(data_ref[boxes, DATA:, :].astype(jnp.float32)) * (1.0 / CODE)
            box_cos[boxes], box_sin[boxes] = cos_sin(phase)
        else:
            pair = data_ref[boxes, 2 * SLAB * part : 2 * SLAB * (part + 1), :].astype(jnp.float32)
            for i in range(2):
                piece = pair[:, i * SLAB : (i + 1) * SLAB, :]
                current[block * HALF : (block + 1) * HALF, strip(2 * part + i)] = piece.reshape(
                    HALF, STRIP
                )

    def turn(k, j, slabs):
        node_cos, node_sin = own_cos[k, :, strip(j)], own_sin[k, :, strip(j)]
        at = slice(SLAB * j + k - 1, SLAB * j + k)
        re_parts, im_parts = [], []
        for slab in slabs:
            if k:
                c, s = box_cos[slab, at, :], box_sin[slab, at, :]
                cosine = c * node_cos - s * node_sin
                sine = s * node_cos + c * node_sin
            else:
                cosine, sine = node_cos, node_sin
            rows = slice(slab * SLAB, (slab + 1) * SLAB)
            re, im = current[rows, strip(j)], current[rows, strip(2 + j)]
            re_parts.append(re * cosine - im * sine)
            im_parts.append(re * sine + im * cosine)
        return jnp.concatenate(re_parts, axis=0), jnp.concatenate(im_parts, axis=0)

    def rotate_within(k, block, i, j):
        first = (block * HALF + i * CHUNK) // SLAB
        sides = [
            turn(k, j, range(first + side, first + side + SLAB)) for side in (0, BLOCK // SLAB)
        ]
        mix_within(1 + k, block, i, j, sides, mixed)

    def rotate_slabs(k, block, half, i, j):
        slabs = pair_slabs(BOX_BITS[k - WITHIN], half, SPLITS[k - WITHIN], block)[i : i + SLAB]
        first = block * BLOCK + i * SLAB
        to = slice(first, first + CHUNK)
        for part, turned in enumerate(turn(k, j, slabs)):
            mixed[to, strip(4 * half + 2 * part + j)] = turned.astype(jnp.bfloat16)

    def rotate(k, block):
        if k >= WITHIN:
            return [
                functools.partial(rotate_slabs, k, block, half, i, j)
                for half in range(2)
                for i in range(0, BLOCK // SLAB, SLAB)
                for j in range(2)
            ]
        steps = [
            functools.partial(rotate_within, k, block, i, j)
            for i in range(BLOCK // CHUNK)
            for j in range(2)
        ]
        if k:
            return steps
        steps = [functools.partial(receive, block, part) for part in range(3)] + steps
        return steps + rotate(0, 1) if block == 0 else steps

    def multiply(k, block):
        target = out_ref if k == INNER - 1 else current
        if block == 0 and k in (0, WITHIN, WITHIN + 1):
            copies[max(k - 1, 0)].wait()
        if k < WITHIN:
            steps = [
                functools.partial(
                    multiply_within, 1 + k, block, part, current, mixed, weights.at[0]
                )
                for part in range(2)
            ]
            return [copies[1 + block].start] + steps if k == 0 else steps
        return [
            functools.partial(
                multiply_part, BOX_BITS[k - WITHIN], SPLITS[k - WITHIN], block, part, target, mixed,
                weights.at[1 + SECOND[k - WITHIN]],
            )
            for part in range(4)
        ]

    def rotate_later(k, block):
        return [] if (k, block) == (0, 1) else rotate(k, block)

    pipeline(INNER, rotate_later, multiply, apart=[(5, 0)])


def inner_levels(*operands):
    return pl.pallas_call(
        inner_kernel,
        in_specs=[VMEM] * 3 + [HBM] * 3,
        out_specs=VMEM,
        out_shape=jax.ShapeDtypeStruct((ROWS, WIDTH), jnp.bfloat16),
        scratch_shapes=[
            pltpu.VMEM((ROWS, WIDTH), jnp.float32),
            pltpu.VMEM((ROWS // 2, 2 * WIDTH), jnp.bfloat16),
            pltpu.VMEM((BOXES, 2 * SLAB, STRIP), jnp.float32),
            pltpu.VMEM((BOXES, 2 * SLAB, STRIP), jnp.float32),
            pltpu.VMEM((3, 2 * WIDTH, 2 * WIDTH), jnp.bfloat16),
            DMA((3,)),
        ],
        compiler_params=pltpu.CompilerParams(vmem_limit_bytes=50 << 20),
        cost_estimate=pl.CostEstimate(flops=9 << 30, bytes_accessed=8 << 20, transcendentals=0),
        name="levels1to9",
    )(*operands)


def outer_kernel(
    data_ref, cos_ref, sin_ref, weight, out_hbm, current, mixed, result, sems
):
    def receive(block):
        rows = slice(block * HALF, (block + 1) * HALF)
        current[rows] = data_ref[rows].astype(jnp.float32)

    leaving = [
        pltpu.make_async_copy(
            result.at[pl.ds(block * HALF, HALF)],
            out_hbm.at[pl.ds(block * HALF, HALF)],
            sems.at[block],
        )
        for block in range(2)
    ]

    def rotate_slabs(k, block, half, i):
        slabs = pair_slabs(k, half, SPLIT, block)[i : i + SLAB]
        first = block * BLOCK + i * SLAB
        at = half * HALF + first
        rotate_into(
            mixed,
            slice(first, first + CHUNK),
            half,
            load_slabs(current, slabs, RE),
            load_slabs(current, slabs, IM),
            cos_ref[k, at : at + CHUNK, :].astype(jnp.float32),
            sin_ref[k, at : at + CHUNK, :].astype(jnp.float32),
        )

    def rotate(k, block):
        arrive = [functools.partial(receive, block)] if k == 0 else []
        return arrive + [
            functools.partial(rotate_slabs, k, block, half, i)
            for half in range(2)
            for i in range(0, BLOCK // SLAB, SLAB)
        ]

    def multiply(k, block):
        target = result if k == 2 else current
        parts = [
            functools.partial(multiply_part, k, SPLIT, block, part, target, mixed, weight)
            for part in range(4)
        ]
        return parts + [leaving[block].start] if k == 2 else parts

    pipeline(3, rotate, multiply)
    for copy in leaving:
        copy.wait()


def outer_levels(*operands):
    return pl.pallas_call(
        outer_kernel,
        in_specs=[VMEM] * len(operands),
        out_specs=HBM,
        out_shape=jax.ShapeDtypeStruct((ROWS, WIDTH), jnp.bfloat16),
        scratch_shapes=[
            pltpu.VMEM((ROWS, WIDTH), jnp.float32),
            pltpu.VMEM((ROWS // 2, 2 * WIDTH), jnp.bfloat16),
            pltpu.VMEM((ROWS, WIDTH), jnp.bfloat16),
            DMA((2,)),
        ],
        compiler_params=pltpu.CompilerParams(vmem_limit_bytes=32 << 20),
        cost_estimate=pl.CostEstimate(flops=3 << 30, bytes_accessed=8 << 20, transcendentals=0),
        name="levels10to12",
    )(*operands)


def exchange(blocks):
    return lax.all_to_all(blocks, AXES, 0, 0, tiled=True)


def on_device(signal, box_phase, node_phase, local_interp, across_x, across_y):
    own = box_phase[:, 0]
    moved = exchange(first_levels(signal[0, 0], own, node_phase, local_interp))
    last_cos, last_sin, own_cos, own_sin, local, *weights = prep(
        own, node_phase, local_interp, across_x, across_y
    )
    inner = inner_levels(moved, own_cos, own_sin, *weights)
    return outer_levels(exchange(inner), last_cos, last_sin, local)[None, None]


def solution(mesh):
    return jax.shard_map(
        on_device,
        mesh=mesh,
        in_specs=(P("sx", "sy", None, None), P(None, "sx", "sy", None), P(), P(), P(), P()),
        out_specs=P("sx", "sy", None, None),
        check_vma=False,
    )
```

profile of v0, /device:TPU:1, one launch (start us, length us, event | category | flops | bytes accessed | tf_op | source)
XLA Modules:
  0.0 83.3 jit_solution(12387277472333191245)
XLA Ops:
  0.0 5.6 %level0.1 = bf16[128,48,128]{2,1,0:T(8,128)(2,1)} custom-call(bf16[1024,512]{1,0:T(8,128)(2,1)} %bitcast.9, f32[13,1,256]{2,1,0:T(1,128)} %bitcast.7, f32[13,1024,256]{2,1,0:T(8,128)} %node_hbm.3, bf16[2,2,2,256,256]{4,3,2,1,0:T(8,128)(2,1)} %local_hbm.1), custom_call_target="tpu_custom_call" | custom-call | flops 1073741824 | bytes 8388608 | tf_op jit(solution)/shard_map/level0/pallas_call | solution.py:248
  5.6 0.0 copy-start
  5.6 0.0 copy-start.1
  5.6 11.5 %all-to-all-start = ((bf16[128,48,128]{2,1,0:T(8,128)(2,1)}), bf16[128,48,128]{2,1,0:T(8,128)(2,1)S(1)}, u32[]{:S(2)}, u32[]{:S(2)}) async-start(bf16[128,48,128]{2,1,0:T(8,128)(2,1)} %level0.1), calls=%async_computation | async-start | bytes 3145728 | tf_op jit(solution)/shard_map/all_to_all | solution.py:524
  17.1 0.0 copy-done
  17.1 0.0 copy-done.1
  17.1 10.0 %prep.1 = (bf16[3,1024,256]{2,1,0:T(8,128)(2,1)}, bf16[3,1024,256]{2,1,0:T(8,128)(2,1)}, f32[9,8,256]{2,1,0:T(8,128)S(1)}, f32[9,8,256]{2,1,0:T(8,128)S(1)}, bf1...) custom-call(f32[13,1,256]{2,1,0:T(1,128)S(1)} %bitcast.8, ...), custom_call_target="tpu_custom_call" | custom-call | flops 60000000 | bytes 7340032 | tf_op jit(solution)/shard_map/prep/pallas_call | solution.py:313
  27.1 14.3 %all-to-all-done.data_ref = bf16[128,48,128]{2,1,0:T(8,128)(2,1)S(1)} async-done(((bf16[128,48,128]{2,1,0:T(8,128)(2,1)}), bf16[128,48,128]{2,1,0:T(8,128)(2,1)S(1)}, u32[]{:S(2)}, u32[]{:S(2)}) %all-to-all-start) | async-done | bytes 1572896 | tf_op jit(solution)/shard_map/all_to_all | solution.py:524
  41.4 0.0 copy-start.3
  41.4 0.0 copy-start.4
  41.4 13.8 %levels1to9.1 = bf16[1024,512]{1,0:T(8,128)(2,1)S(1)} custom-call(bf16[128,48,128]{2,1,0:T(8,128)(2,1)S(1)} %all-to-all-done.data_ref, f32[9,8,256]{2,1,0:T(8,128)S(1)} %get-tuple-element.13.own_cos, f32[9,8,256]{2,1,0:T(8,128)S(1)} %get-tuple-element.14.own_sin, bf16[1024,1024]{1,0:T(8,128)(2,1)} %get-tuple-element.15.local_hbm, ...), custom_call_target="tpu_custom_call" | custom-call | flops 9663676416 | bytes 8388608 | tf_op jit(solution)/shard_map/levels1to9/pallas_call | solution.py:435
  55.2 0.0 copy-start.2
  55.3 23.3 %all_to_all.16 = bf16[128,8,512]{2,1,0:T(8,128)(2,1)S(1)} all-to-all(bf16[128,8,512]{2,1,0:T(8,128)(2,1)S(1)} %bitcast.5), channel_id=1, replica_groups=mesh['sx'=8,'sy'=16] {'sx','sy'}, dimensions={0} | all-to-all | bytes 2097152 | tf_op jit(solution)/shard_map/all_to_all | solution.py:524
  78.6 0.0 copy-done.3
  78.6 0.0 copy-done.4
  78.6 0.0 copy-done.2
  78.6 4.5 %levels10to12.1 = bf16[1024,512]{1,0:T(8,128)(2,1)} custom-call(bf16[1024,512]{1,0:T(8,128)(2,1)S(1)} %bitcast.6, bf16[3,1024,256]{2,1,0:T(8,128)(2,1)S(1)} %copy-done.3, bf16[3,1024,256]{2,1,0:T(8,128)(2,1)S(1)} %copy-done.4, bf16[1024,1024]{1,0:T(8,128)(2,1)S(1)} %copy-done.2), custom_call_target="tpu_custom_call" | custom-call | flops 3221225472 | bytes 8388608 | tf_op jit(solution)/shard_map/levels10to12/pallas_call | solution.py:506
Async XLA Ops:
  5.6 11.5 %copy-start = (bf16[2,2,2,256,256]{4,3,2,1,0:T(8,128)(2,1)S(1)}, bf16[2,2,2,256,256]{4,3,2,1,0:T(8,128)(2,1)}, u32[]{:S(2)}) copy-start(bf16[2,2,2,256,256]{4,3,2,1,0:T(8,128)(2,1)} %local_hbm.1) | copy-start | bytes 3145732
  5.6 11.5 %copy-start.1 = (f32[13,1,1,256]{3,2,1,0:T(1,128)S(1)}, f32[13,1,1,256]{3,2,1,0:T(1,128)}, u32[]{:S(2)}) copy-start(f32[13,1,1,256]{3,2,1,0:T(1,128)} %param.7) | copy-start | bytes 39940
  5.6 35.8 %all-to-all-start = ((bf16[128,48,128]{2,1,0:T(8,128)(2,1)}), bf16[128,48,128]{2,1,0:T(8,128)(2,1)S(1)}, u32[]{:S(2)}, u32[]{:S(2)}) async-start(bf16[128,48,128]{2,1,0:T(8,128)(2,1)} %level0.1), calls=%async_computation | async-start | bytes 3145728 | tf_op jit(solution)/shard_map/all_to_all | solution.py:524
  41.4 37.2 %copy-start.3 = (bf16[3,1024,256]{2,1,0:T(8,128)(2,1)S(1)}, bf16[3,1024,256]{2,1,0:T(8,128)(2,1)}, u32[]{:S(2)}) copy-start(bf16[3,1024,256]{2,1,0:T(8,128)(2,1)} %get-tuple-element.18.cos_ref) | copy-start | bytes 4718596
  41.4 37.2 %copy-start.4 = (bf16[3,1024,256]{2,1,0:T(8,128)(2,1)S(1)}, bf16[3,1024,256]{2,1,0:T(8,128)(2,1)}, u32[]{:S(2)}) copy-start(bf16[3,1024,256]{2,1,0:T(8,128)(2,1)} %get-tuple-element.19.sin_ref) | copy-start | bytes 4718596
  55.2 23.4 %copy-start.2 = (bf16[1024,1024]{1,0:T(8,128)(2,1)S(1)}, bf16[1024,1024]{1,0:T(8,128)(2,1)}, u32[]{:S(2)}) copy-start(bf16[1024,1024]{1,0:T(8,128)(2,1)} %get-tuple-element.20.weight) | copy-start | bytes 6291460
where the time goes:
time: 83.6 us; the launch traced here: 83.3 us
  Pallas kernels  33.9 us (41%)
  blocking collectives  23.3 us (28%)
  waiting for transfers between devices  14.3 us (17%)
  starting transfers between devices  11.5 us (14%)
    all_to_all x1, blocking collectives, exchange(): return lax.all_to_all(blocks, AXES, 0, 0, tiled=True)  23.3 us
    all_to_all x1, waiting for transfers between devices, exchange(): return lax.all_to_all(blocks, AXES, 0, 0, tiled=True)  14.3 us
    pallas_call x1, Pallas kernels, inner_levels(): pl.pallas_call(inner_kernel, in_specs=[VMEM] * 3 + [HBM] * 3, out_specs=V...  13.8 us
    all_to_all x1, starting transfers between devices, exchange(): return lax.all_to_all(blocks, AXES, 0, 0, tiled=True)  11.5 us
    pallas_call x1, Pallas kernels, prep(): pl.pallas_call(prep_kernel, in_specs=[VMEM] + [HBM] * 4, out_specs=[VMEM]...  10 us
    pallas_call x1, Pallas kernels, first_levels(): pl.pallas_call(first_kernel, in_specs=[HBM, VMEM, HBM, HBM], out_specs=HB...  5.56 us
    pallas_call x1, Pallas kernels, outer_levels(): pl.pallas_call(outer_kernel, in_specs=[VMEM] * len(operands), out_specs=H...  4.5 us
  transfers between devices with their start and end apart: 1, of which 1 were waited for; matrix products, arithmetic and copies ran while one was open for 0% of the time, Pallas kernels for 12%

commit v1 on v0

--- a/solution.py
+++ b/solution.py
@@ -107,20 +107,31 @@
 def fill_weight(weight, interp):
     for child in range(2):
         for source in range(2):
-            r, c = source * WIDTH, child * WIDTH
-            real, imag = interp[child, source, 0], interp[child, source, 1]
-            weight[r : r + NODES, c : c + NODES] = real
-            weight[r : r + NODES, c + NODES : c + WIDTH] = imag
-            weight[r + NODES : r + WIDTH, c : c + NODES] = -imag
-            weight[r + NODES : r + WIDTH, c + NODES : c + WIDTH] = real
-
-
-def product(mixed, block, part, weight):
-    return jnp.dot(
-        mixed[block * BLOCK : (block + 1) * BLOCK],
-        weight[:, part * NODES : (part + 1) * NODES],
-        preferred_element_type=jnp.float32,
-    )
+            rows = slice(source * NODES, (source + 1) * NODES)
+            columns = slice(child * NODES, (child + 1) * NODES)
+            real = interp[child, source, 0].astype(jnp.float32)
+            imag = interp[child, source, 1].astype(jnp.float32)
+            for i, factor in enumerate((real, imag - real, imag + real)):
+                weight[i, rows, columns] = factor.astype(jnp.bfloat16)
+
+
+def product(mixed, block, child, weight):
+    rows = slice(block * BLOCK, (block + 1) * BLOCK)
+    both, real, imag = [
+        jnp.dot(
+            mixed[rows, i * WIDTH : (i + 1) * WIDTH],
+            weight[i, :, child * NODES : (child + 1) * NODES],
+            preferred_element_type=jnp.float32,
+        )
+        for i in range(3)
+    ]
+    return jnp.concatenate([both - imag, both + real], axis=1)
+
+
+def keep(mixed, rows, half, column, re, im):
+    for i, values in enumerate((re + im, re, im)):
+        first = i * WIDTH + half * NODES + column
+        mixed[rows, first : first + values.shape[-1]] = values.astype(jnp.bfloat16)
 
 
 def strip(j):
@@ -128,9 +139,7 @@
 
 
 def rotate_into(mixed, rows, half, re, im, c, s):
-    left = half * WIDTH
-    mixed[rows, left : left + NODES] = (re * c - im * s).astype(jnp.bfloat16)
-    mixed[rows, left + NODES : left + WIDTH] = (re * s + im * c).astype(jnp.bfloat16)
+    keep(mixed, rows, half, 0, re * c - im * s, re * s + im * c)
 
 
 def swap(bit, zero, one):
@@ -144,51 +153,63 @@
 
 def mix_within(bit, block, i, j, sides, mixed):
     at = block * BLOCK + i * CHUNK
-    for part in range(2):
-        pair = [side[part].reshape(CHUNK // SLAB, SLAB, STRIP) for side in sides]
-        for half, rows in enumerate(swap(bit, *pair)):
-            mixed[at : at + CHUNK, strip(4 * half + 2 * part + j)] = rows.reshape(
-                CHUNK, STRIP
-            ).astype(jnp.bfloat16)
-
-
-def multiply_within(bit, block, part, target, mixed, weight):
+    swapped = [
+        swap(bit, *[side[part].reshape(CHUNK // SLAB, SLAB, STRIP) for side in sides])
+        for part in range(2)
+    ]
+    for half in range(2):
+        re, im = [swapped[part][half].reshape(CHUNK, STRIP) for part in range(2)]
+        keep(mixed, slice(at, at + CHUNK), half, j * STRIP, re, im)
+
+
+def multiply_within(bit, block, target, mixed, weight):
     pair = [
-        product(mixed, block, 2 * child + part, weight).reshape(BLOCK // SLAB, SLAB, NODES)
+        product(mixed, block, child, weight).reshape(BLOCK // SLAB, SLAB, WIDTH)
         for child in range(2)
     ]
     for side, rows in enumerate(swap(bit, *pair)):
         first = block * HALF + side * BLOCK
-        target[first : first + BLOCK, (RE, IM)[part]] = rows.reshape(BLOCK, NODES)
+        target[first : first + BLOCK] = rows.reshape(BLOCK, WIDTH)
 
 
 def first_kernel(
     data_hbm, box_ref, node_hbm, interp_hbm, out_hbm,
     data, nodes, interp, weight, cosines, sines, current, mixed, messages, sems,
 ):
-    copies = [
-        pltpu.make_async_copy(node_hbm.at[0], nodes, sems.at[0]),
-        pltpu.make_async_copy(interp_hbm, interp, sems.at[1]),
-        pltpu.make_async_copy(data_hbm, data, sems.at[2]),
-    ]
-    for copy in copies:
-        copy.start()
+    halves = [pl.ds(block * HALF, HALF) for block in range(2)]
+    node_copies = [
+        pltpu.make_async_copy(node_hbm.at[0, half], nodes.at[half], sems.at[block])
+        for block, half in enumerate(halves)
+    ]
+    data_copies = [
+        pltpu.make_async_copy(data_hbm.at[half], data.at[half], sems.at[2 + block])
+        for block, half in enumerate(halves)
+    ]
+    interp_copy = pltpu.make_async_copy(interp_hbm, interp, sems.at[4])
+    node_copies[0].start()
+    interp_copy.start()
+    data_copies[0].start()
+    node_copies[1].start()
+    data_copies[1].start()
     box_cos, box_sin = cos_sin(box_ref[0])
     next_cos, next_sin = cos_sin(box_ref[1])
     phases = [box_ref[FIRST + 1 + k][:, strip(j)] for j in range(2) for k in range(SLAB)]
     code = jnp.exp2(jnp.concatenate(phases, axis=0) * CODE).astype(jnp.bfloat16)
     messages[:, DATA:, :] = jnp.broadcast_to(code[None], (BOXES, 2 * SLAB, STRIP))
-    copies[0].wait()
-    for first in range(0, ROWS, CHUNK):
+
+    def form(first, j):
+        rows, columns = slice(first, first + CHUNK), strip(j)
+        node_cos, node_sin = cos_sin(nodes[rows, columns])
+        c, s = box_cos[:, columns], box_sin[:, columns]
+        cosines[rows, columns] = node_cos * c - node_sin * s
+        sines[rows, columns] = node_sin * c + node_cos * s
+
+    node_copies[0].wait()
+    for first in range(0, HALF, CHUNK):
         for j in range(2):
-            rows, columns = slice(first, first + CHUNK), strip(j)
-            node_cos, node_sin = cos_sin(nodes[rows, columns])
-            c, s = box_cos[:, columns], box_sin[:, columns]
-            cosines[rows, columns] = node_cos * c - node_sin * s
-            sines[rows, columns] = node_sin * c + node_cos * s
-    copies[1].wait()
+            form(first, j)
+    interp_copy.wait()
     fill_weight(weight, interp)
-    copies[2].wait()
 
     def rotate_rows(block, i, j):
         sides = []
@@ -202,11 +223,21 @@
         mix_within(0, block, i, j, sides, mixed)
 
     def rotate(k, block):
-        return [
+        data_copies[block].wait()
+        steps = [
             functools.partial(rotate_rows, block, i, j)
             for i in range(BLOCK // CHUNK)
             for j in range(2)
         ]
+        if block == 0:
+            return steps
+        node_copies[1].wait()
+        forms = [
+            functools.partial(form, first, j)
+            for first in range(HALF, ROWS, CHUNK)
+            for j in range(2)
+        ]
+        return forms + steps
 
     def pack(block, i):
         first = block * HALF + i * CHUNK
@@ -222,22 +253,23 @@
                 pair, axis=1
             ).astype(jnp.bfloat16)
 
+    batch = 2 * CHUNK // SLAB
     leaving = [
         pltpu.make_async_copy(
-            messages.at[pl.ds(block * CHUNK, CHUNK)],
-            out_hbm.at[pl.ds(block * CHUNK, CHUNK)],
-            sems.at[3 + block],
+            messages.at[pl.ds(first, batch)], out_hbm.at[pl.ds(first, batch)], sems.at[5 + i]
         )
-        for block in range(2)
+        for i, first in enumerate(range(0, BOXES, batch))
     ]
 
     def multiply(k, block):
         steps = [
-            functools.partial(multiply_within, 0, block, part, current, mixed, weight)
-            for part in range(2)
-        ]
-        steps += [functools.partial(pack, block, i) for i in range(HALF // CHUNK)]
-        return steps + [leaving[block].start]
+            functools.partial(multiply_within, 0, block, current, mixed, weight)
+        ]
+        for i in range(HALF // CHUNK):
+            steps.append(functools.partial(pack, block, i))
+            if i % 2:
+                steps.append(leaving[(block * (HALF // CHUNK) + i) // 2].start)
+        return steps
 
     pipeline(1, rotate, multiply)
     for copy in leaving:
@@ -254,13 +286,13 @@
             pltpu.VMEM((ROWS, WIDTH), jnp.bfloat16),
             pltpu.VMEM((ROWS, NODES), jnp.float32),
             pltpu.VMEM((2, 2, 2, NODES, NODES), jnp.bfloat16),
-            pltpu.VMEM((2 * WIDTH, 2 * WIDTH), jnp.bfloat16),
+            pltpu.VMEM((3, WIDTH, WIDTH), jnp.bfloat16),
             pltpu.VMEM((ROWS, NODES), jnp.float32),
             pltpu.VMEM((ROWS, NODES), jnp.float32),
             pltpu.VMEM((ROWS, WIDTH), jnp.float32),
-            pltpu.VMEM((ROWS // 2, 2 * WIDTH), jnp.bfloat16),
+            pltpu.VMEM((ROWS // 2, 3 * WIDTH), jnp.bfloat16),
             pltpu.VMEM((BOXES, MESSAGE, STRIP), jnp.bfloat16),
-            DMA((5,)),
+            DMA((13,)),
         ],
         compiler_params=pltpu.CompilerParams(vmem_limit_bytes=58 << 20),
         cost_estimate=pl.CostEstimate(flops=1 << 30, bytes_accessed=8 << 20, transcendentals=0),
@@ -270,7 +302,7 @@
 
 def prep_kernel(
     box_ref, node_hbm, local_hbm, x_hbm, y_hbm,
-    cos_ref, sin_ref, own_cos, own_sin, local_weight, inner_weight, x_weight, y_weight,
+    cos_ref, sin_ref, own_cos, own_sin, local_weight, inner_weights,
     own, nodes, interps, sems,
 ):
     me = lax.axis_index("sx") * lax.axis_size("sy") + lax.axis_index("sy")
@@ -286,10 +318,10 @@
         copy.start()
     copies[0].wait()
     own_cos[...], own_sin[...] = cos_sin(own[...])
-    for k, weight in enumerate((x_weight, y_weight, local_weight)):
+    for k in range(3):
         copies[4 + k].wait()
-        fill_weight(weight, interps.at[k])
-    fill_weight(inner_weight, interps.at[2])
+        fill_weight(inner_weights.at[(k + 1) % 3], interps.at[k])
+    fill_weight(local_weight, interps.at[2])
     for k in range(3):
         copies[1 + k].wait()
         box_cos, box_sin = cos_sin(box_ref[LAST + k])
@@ -307,14 +339,15 @@
 
 
 def prep(box_phase, node_phase, *interps):
-    weight = jax.ShapeDtypeStruct((2 * WIDTH, 2 * WIDTH), jnp.bfloat16)
+    weight = jax.ShapeDtypeStruct((3, WIDTH, WIDTH), jnp.bfloat16)
+    weights = jax.ShapeDtypeStruct((3, 3, WIDTH, WIDTH), jnp.bfloat16)
     table = jax.ShapeDtypeStruct((3, ROWS, NODES), jnp.bfloat16)
     own = jax.ShapeDtypeStruct((INNER, SLAB, NODES), jnp.float32)
     return pl.pallas_call(
         prep_kernel,
         in_specs=[VMEM] + [HBM] * 4,
-        out_specs=[VMEM] * 8,
-        out_shape=[table, table, own, own, weight, weight, weight, weight],
+        out_specs=[VMEM] * 6,
+        out_shape=[table, table, own, own, weight, weights],
         scratch_shapes=[
             pltpu.VMEM((INNER, SLAB, NODES), jnp.float32),
             pltpu.VMEM((3, ROWS, NODES), jnp.float32),
@@ -327,19 +360,18 @@
     )(box_phase, node_phase, *interps)
 
 
-def multiply_part(bit, split, block, part, target, mixed, weight):
-    total = product(mixed, block, part, weight)
-    for at, r, n in runs(pair_slabs(bit, part >> 1, split, block)):
-        target[r : r + n, (RE, IM)[part & 1]] = total[at : at + n].astype(target.dtype)
+def multiply_child(bit, split, block, child, target, mixed, weight):
+    total = product(mixed, block, child, weight)
+    for at, r, n in runs(pair_slabs(bit, child, split, block)):
+        target[r : r + n] = total[at : at + n].astype(target.dtype)
 
 
 def inner_kernel(
-    data_ref, own_cos, own_sin, local_hbm, x_hbm, y_hbm, out_ref,
+    data_ref, own_cos, own_sin, weights_hbm, out_ref,
     current, mixed, box_cos, box_sin, weights, sems,
 ):
     copies = [
-        pltpu.make_async_copy(hbm, weights.at[i], sems.at[i])
-        for i, hbm in enumerate((local_hbm, x_hbm, y_hbm))
+        pltpu.make_async_copy(weights_hbm.at[i], weights.at[i], sems.at[i]) for i in range(3)
     ]
     copies[0].start()
 
@@ -384,8 +416,7 @@
         slabs = pair_slabs(BOX_BITS[k - WITHIN], half, SPLITS[k - WITHIN], block)[i : i + SLAB]
         first = block * BLOCK + i * SLAB
         to = slice(first, first + CHUNK)
-        for part, turned in enumerate(turn(k, j, slabs)):
-            mixed[to, strip(4 * half + 2 * part + j)] = turned.astype(jnp.bfloat16)
+        keep(mixed, to, half, j * STRIP, *turn(k, j, slabs))
 
     def rotate(k, block):
         if k >= WITHIN:
@@ -412,17 +443,16 @@
         if k < WITHIN:
             steps = [
                 functools.partial(
-                    multiply_within, 1 + k, block, part, current, mixed, weights.at[0]
+                    multiply_within, 1 + k, block, current, mixed, weights.at[0]
                 )
-                for part in range(2)
             ]
             return [copies[1 + block].start] + steps if k == 0 else steps
         return [
             functools.partial(
-                multiply_part, BOX_BITS[k - WITHIN], SPLITS[k - WITHIN], block, part, target, mixed,
-                weights.at[1 + SECOND[k - WITHIN]],
+                multiply_child, BOX_BITS[k - WITHIN], SPLITS[k - WITHIN], block, child, target,
+                mixed, weights.at[1 + SECOND[k - WITHIN]],
             )
-            for part in range(4)
+            for child in range(2)
         ]
 
     def rotate_later(k, block):
@@ -434,15 +464,15 @@
 def inner_levels(*operands):
     return pl.pallas_call(
         inner_kernel,
-        in_specs=[VMEM] * 3 + [HBM] * 3,
+        in_specs=[VMEM] * 3 + [HBM],
         out_specs=VMEM,
         out_shape=jax.ShapeDtypeStruct((ROWS, WIDTH), jnp.bfloat16),
         scratch_shapes=[
             pltpu.VMEM((ROWS, WIDTH), jnp.float32),
-            pltpu.VMEM((ROWS // 2, 2 * WIDTH), jnp.bfloat16),
+            pltpu.VMEM((ROWS // 2, 3 * WIDTH), jnp.bfloat16),
             pltpu.VMEM((BOXES, 2 * SLAB, STRIP), jnp.float32),
             pltpu.VMEM((BOXES, 2 * SLAB, STRIP), jnp.float32),
-            pltpu.VMEM((3, 2 * WIDTH, 2 * WIDTH), jnp.bfloat16),
+            pltpu.VMEM((3, 3, WIDTH, WIDTH), jnp.bfloat16),
             DMA((3,)),
         ],
         compiler_params=pltpu.CompilerParams(vmem_limit_bytes=50 << 20),
@@ -492,8 +522,8 @@
     def multiply(k, block):
         target = result if k == 2 else current
         parts = [
-            functools.partial(multiply_part, k, SPLIT, block, part, target, mixed, weight)
-            for part in range(4)
+            functools.partial(multiply_child, k, SPLIT, block, child, target, mixed, weight)
+            for child in range(2)
         ]
         return parts + [leaving[block].start] if k == 2 else parts
 
@@ -510,7 +540,7 @@
         out_shape=jax.ShapeDtypeStruct((ROWS, WIDTH), jnp.bfloat16),
         scratch_shapes=[
             pltpu.VMEM((ROWS, WIDTH), jnp.float32),
-            pltpu.VMEM((ROWS // 2, 2 * WIDTH), jnp.bfloat16),
+            pltpu.VMEM((ROWS // 2, 3 * WIDTH), jnp.bfloat16),
             pltpu.VMEM((ROWS, WIDTH), jnp.bfloat16),
             DMA((2,)),
         ],
@@ -527,10 +557,10 @@
 def on_device(signal, box_phase, node_phase, local_interp, across_x, across_y):
     own = box_phase[:, 0]
     moved = exchange(first_levels(signal[0, 0], own, node_phase, local_interp))
-    last_cos, last_sin, own_cos, own_sin, local, *weights = prep(
+    last_cos, last_sin, own_cos, own_sin, local, weights = prep(
         own, node_phase, local_interp, across_x, across_y
     )
-    inner = inner_levels(moved, own_cos, own_sin, *weights)
+    inner = inner_levels(moved, own_cos, own_sin, weights)
     return outer_levels(exchange(inner), last_cos, last_sin, local)[None, None]
 
 

time: 83.6 us -> 81.1 us (0.970)
  Pallas kernels: 33.9 us -> 30.2 us
  waiting for transfers between devices: 14.3 us -> 15.4 us
    pallas_call x1, Pallas kernels: 13.8 us -> 12.1 us  [inner_levels(): pl.pallas_call(inner_kernel, in_specs=[VMEM] * 3 + [HBM], out_specs=VMEM,...]
    pallas_call x1, Pallas kernels: 10 us -> 8.82 us  [prep(): pl.pallas_call(prep_kernel, in_specs=[VMEM] + [HBM] * 4, out_specs=[VMEM]...]
    all_to_all x1, waiting for transfers between devices: 14.3 us -> 15.4 us  [exchange(): return lax.all_to_all(blocks, AXES, 0, 0, tiled=True)]
  transfers between devices with their start and end apart: 1 -> 1, of which waited for: 1 -> 1; matrix products, arithmetic and copies ran while one was open for 0% -> 0% of each run, Pallas kernels for 12% -> 11%
where the time goes in v1:
time: 81.1 us; the launch traced here: 80.8 us
  Pallas kernels  30.2 us (37%)
  blocking collectives  23.3 us (29%)
  waiting for transfers between devices  15.4 us (19%)
  starting transfers between devices  11.5 us (14%)
    all_to_all x1, blocking collectives, exchange(): return lax.all_to_all(blocks, AXES, 0, 0, tiled=True)  23.3 us
    all_to_all x1, waiting for transfers between devices, exchange(): return lax.all_to_all(blocks, AXES, 0, 0, tiled=True)  15.4 us
    pallas_call x1, Pallas kernels, inner_levels(): pl.pallas_call(inner_kernel, in_specs=[VMEM] * 3 + [HBM], out_specs=VMEM,...  12.1 us
    all_to_all x1, starting transfers between devices, exchange(): return lax.all_to_all(blocks, AXES, 0, 0, tiled=True)  11.5 us
    pallas_call x1, Pallas kernels, prep(): pl.pallas_call(prep_kernel, in_specs=[VMEM] + [HBM] * 4, out_specs=[VMEM]...  8.82 us
    pallas_call x1, Pallas kernels, first_levels(): pl.pallas_call(first_kernel, in_specs=[HBM, VMEM, HBM, HBM], out_specs=HB...  5.6 us
    pallas_call x1, Pallas kernels, outer_levels(): pl.pallas_call(outer_kernel, in_specs=[VMEM] * len(operands), out_specs=H...  3.73 us
  transfers between devices with their start and end apart: 1, of which 1 were waited for; matrix products, arithmetic and copies ran while one was open for 0% of the time, Pallas kernels for 11%

profile of v1, /device:TPU:1, one launch (start us, length us, event | category | flops | bytes accessed | tf_op | source)
XLA Modules:
  0.0 80.8 jit_solution(12619796825419104607)
XLA Ops:
  0.0 5.6 %level0.1 = bf16[128,48,128]{2,1,0:T(8,128)(2,1)} custom-call(bf16[1024,512]{1,0:T(8,128)(2,1)} %bitcast.9, f32[13,1,256]{2,1,0:T(1,128)} %bitcast.7, f32[13,1024,256]{2,1,0:T(8,128)} %node_hbm.3, bf16[2,2,2,256,256]{4,3,2,1,0:T(8,128)(2,1)} %local_hbm.1), custom_call_target="tpu_custom_call" | custom-call | flops 1073741824 | bytes 8388608 | tf_op jit(solution)/shard_map/level0/pallas_call | solution.py:280
  5.6 0.0 copy-start
  5.6 0.0 copy-start.1
  5.6 11.5 %all-to-all-start = ((bf16[128,48,128]{2,1,0:T(8,128)(2,1)}), bf16[128,48,128]{2,1,0:T(8,128)(2,1)S(1)}, u32[]{:S(2)}, u32[]{:S(2)}) async-start(bf16[128,48,128]{2,1,0:T(8,128)(2,1)} %level0.1), calls=%async_computation | async-start | bytes 3145728 | tf_op jit(solution)/shard_map/all_to_all | solution.py:554
  17.1 0.0 copy-done
  17.2 0.0 copy-done.1
  17.2 8.8 %prep.1 = (bf16[3,1024,256]{2,1,0:T(8,128)(2,1)}, bf16[3,1024,256]{2,1,0:T(8,128)(2,1)}, f32[9,8,256]{2,1,0:T(8,128)S(1)}, f32[9,8,256]{2,1,0:T(8,128)S(1)}, bf1...) custom-call(f32[13,1,256]{2,1,0:T(1,128)S(1)} %bitcast.8, f32[13,1024,256]{2,1,0:T(8,128)} %node_hbm.3, ...), custom_call_target="tpu_custom_call" | custom-call | flops 60000000 | bytes 7340032 | tf_op jit(solution)/shard_map/prep/pallas_call | solution.py:346
  26.0 15.4 %all-to-all-done.data_ref = bf16[128,48,128]{2,1,0:T(8,128)(2,1)S(1)} async-done(((bf16[128,48,128]{2,1,0:T(8,128)(2,1)}), bf16[128,48,128]{2,1,0:T(8,128)(2,1)S(1)}, u32[]{:S(2)}, u32[]{:S(2)}) %all-to-all-start) | async-done | bytes 1572896 | tf_op jit(solution)/shard_map/all_to_all | solution.py:554
  41.4 0.0 copy-start.3
  41.4 0.0 copy-start.4
  41.4 12.1 %levels1to9.1 = bf16[1024,512]{1,0:T(8,128)(2,1)S(1)} custom-call(bf16[128,48,128]{2,1,0:T(8,128)(2,1)S(1)} %all-to-all-done.data_ref, f32[9,8,256]{2,1,0:T(8,128)S(1)} %get-tuple-element.11.own_cos, f32[9,8,256]{2,1,0:T(8,128)S(1)} %get-tuple-element.12.own_sin, bf16[3,3,512,512]{3,2,1,0:T(8,128)(2,1)} %get-tuple-element.13.weights_hbm), custom_call_target="tpu_custom_call" | custom-call | flops 9663676416 | bytes 8388608 | tf_op jit(solution)/shard_map/levels1to9/pallas_call | solution.py:465
  53.5 0.0 copy-start.2
  53.5 23.3 %all_to_all.16 = bf16[128,8,512]{2,1,0:T(8,128)(2,1)S(1)} all-to-all(bf16[128,8,512]{2,1,0:T(8,128)(2,1)S(1)} %bitcast.6), channel_id=1, replica_groups=mesh['sx'=8,'sy'=16] {'sx','sy'}, dimensions={0} | all-to-all | bytes 2097152 | tf_op jit(solution)/shard_map/all_to_all | solution.py:554
  76.8 0.0 copy-done.3
  76.8 0.0 copy-done.4
  76.9 0.0 copy-done.2
  76.9 3.7 %levels10to12.1 = bf16[1024,512]{1,0:T(8,128)(2,1)} custom-call(bf16[1024,512]{1,0:T(8,128)(2,1)S(1)} %bitcast.5, bf16[3,1024,256]{2,1,0:T(8,128)(2,1)S(1)} %copy-done.2, bf16[3,1024,256]{2,1,0:T(8,128)(2,1)S(1)} %copy-done.3, bf16[3,512,512]{2,1,0:T(8,128)(2,1)S(1)} %copy-done.4), custom_call_target="tpu_custom_call" | custom-call | flops 3221225472 | bytes 8388608 | tf_op jit(solution)/shard_map/levels10to12/pallas_call | solution.py:536
Async XLA Ops:
  5.6 11.5 %copy-start = (bf16[2,2,2,256,256]{4,3,2,1,0:T(8,128)(2,1)S(1)}, bf16[2,2,2,256,256]{4,3,2,1,0:T(8,128)(2,1)}, u32[]{:S(2)}) copy-start(bf16[2,2,2,256,256]{4,3,2,1,0:T(8,128)(2,1)} %local_hbm.1) | copy-start | bytes 3145732
  5.6 11.5 %copy-start.1 = (f32[13,1,1,256]{3,2,1,0:T(1,128)S(1)}, f32[13,1,1,256]{3,2,1,0:T(1,128)}, u32[]{:S(2)}) copy-start(f32[13,1,1,256]{3,2,1,0:T(1,128)} %param.7) | copy-start | bytes 39940
  5.6 35.8 %all-to-all-start = ((bf16[128,48,128]{2,1,0:T(8,128)(2,1)}), bf16[128,48,128]{2,1,0:T(8,128)(2,1)S(1)}, u32[]{:S(2)}, u32[]{:S(2)}) async-start(bf16[128,48,128]{2,1,0:T(8,128)(2,1)} %level0.1), calls=%async_computation | async-start | bytes 3145728 | tf_op jit(solution)/shard_map/all_to_all | solution.py:554
  41.4 35.4 %copy-start.3 = (bf16[3,1024,256]{2,1,0:T(8,128)(2,1)S(1)}, bf16[3,1024,256]{2,1,0:T(8,128)(2,1)}, u32[]{:S(2)}) copy-start(bf16[3,1024,256]{2,1,0:T(8,128)(2,1)} %get-tuple-element.15.sin_ref) | copy-start | bytes 4718596
  41.4 35.4 %copy-start.4 = (bf16[3,512,512]{2,1,0:T(8,128)(2,1)S(1)}, bf16[3,512,512]{2,1,0:T(8,128)(2,1)}, u32[]{:S(2)}) copy-start(bf16[3,512,512]{2,1,0:T(8,128)(2,1)} %get-tuple-element.16.weight) | copy-start | bytes 4718596
  53.5 23.3 %copy-start.2 = (bf16[3,1024,256]{2,1,0:T(8,128)(2,1)S(1)}, bf16[3,1024,256]{2,1,0:T(8,128)(2,1)}, u32[]{:S(2)}) copy-start(bf16[3,1024,256]{2,1,0:T(8,128)(2,1)} %get-tuple-element.14.cos_ref) | copy-start | bytes 4718596
